TPU v7x, 512 devices: a whole 4x8x8 slice. The times are simulated.
512 devices in a mesh: seq: 32 (over y, x), head: 16 (over z, core).
Axes of the slice: x: 4, y: 8, z: 8, core: 2. Of those that a mesh axis runs over, the one named last changes fastest.
Arguments:
- queries: bfloat16 [2048, 8192], P('seq', 'head'), may hold values from -6 to 6
- keys: bfloat16 [2048, 1024], P('seq'), may hold values from -6 to 6
- values: bfloat16 [2048, 1024], P('seq'), may hold values from -6 to 6
- vertical: int32 [64, 8], replicated, may hold values from -1 to 31, as said below
- slash: int32 [64, 8], replicated, may hold values from -1 to 31, as said below
- plan: int32 [64], replicated, may hold values from 0 to 63, each once
Outputs:
- attended: bfloat16 [2048, 8192], P('seq', 'head')
Inputs may be any that keep to these rules, and one draw needn't show every extreme that they name: `vertical`: entries of 0 or more name key blocks of 64 positions; -1 marks an unused entry, and every row has at least one used entry. `slash`: entries of 0 or more are offsets back from a query's own block; -1 marks an unused entry; the first entry of every row is 0. `plan`: A permutation of the query heads.
All inputs are finite; a program needn't handle non-finite values.
Results may differ from a plain program's by a relative error of at most 0.0044.
Values may be sent and summed in bfloat16 or wider, within the bound.
A program may use at most 64 MiB of HBM per device.

v0:
```python
import jax
import jax.numpy as jnp
from jax import lax
from jax.sharding import PartitionSpec as P

HD = 128
QH = 64
KVH = 8
BLK = 64


floor_value = -1e30


def block_mask(query_blocks, key_blocks, vertical_rows, slash_rows, query_pos, key_pos):
    vertical_hit = jnp.any(vertical_rows[:, :, None] == key_blocks[None, None, :], axis=1)
    distance = query_blocks[:, None] - key_blocks[None, :]
    slash_hit = jnp.zeros((slash_rows.shape[0],) + distance.shape, jnp.bool_)
    for column in range(slash_rows.shape[1]):
        slash_hit = slash_hit | (slash_rows[:, column][:, None, None] == distance[None])
    causal = key_pos[None, :] <= query_pos[:, None]
    return causal[None] & (vertical_hit[:, None, :] | slash_hit)


def attend(carried, query_group, key_group, value_group, allowed, score_scale):
    max_old, totals_old, sums_old = carried
    scores = (
        jnp.einsum("qgh,kgh->gqk", query_group, key_group, preferred_element_type=jnp.float32)
        * score_scale
    )
    masked = jnp.where(allowed, scores, floor_value)
    max_new = jnp.maximum(max_old, jnp.max(masked, axis=2))
    weights = jnp.exp(masked - max_new[:, :, None])
    totals_new = jnp.sum(weights, axis=2)
    mixture = jnp.einsum(
        "gqk,kgh->qgh",
        weights.astype(jnp.bfloat16),
        value_group,
        preferred_element_type=jnp.float32,
    )
    return (max_new, totals_new, mixture)


def per_device(queries, keys, values, vertical, slash, plan):
    slot_count = plan.shape[0] // lax.axis_size("head")
    query_len = queries.shape[0]
    key_len = keys.shape[0]
    group_size = QH // KVH
    my_heads = lax.dynamic_slice_in_dim(plan, lax.axis_index("head") * slot_count, slot_count)
    kv_index = my_heads // group_size
    slot_column = jnp.arange(slot_count, dtype=jnp.int32)
    key_pick = jnp.take(keys.reshape(key_len, KVH, HD), kv_index, axis=1).reshape(
        key_len, slot_count * HD
    )
    value_pick = jnp.take(values.reshape(key_len, KVH, HD), kv_index, axis=1).reshape(
        key_len, slot_count * HD
    )
    gathered = lax.all_gather(queries, "head", axis=1, tiled=True)
    query_sel = jnp.take(gathered.reshape(query_len, QH, HD), my_heads, axis=1)
    vertical_sel = jnp.take(vertical, my_heads, axis=0)
    slash_sel = jnp.take(slash, my_heads, axis=0)
    query_pos = lax.axis_index("seq") * query_len + jnp.arange(query_len, dtype=jnp.int32)
    query_blocks = query_pos // BLK
    score_scale = HD ** (-0.5)

    def select_rows(rows):
        return jnp.take(rows.reshape(rows.shape[0], slot_count, HD), slot_column, axis=1)

    initial = (
        jnp.full((slot_count, query_len), floor_value, jnp.float32),
        jnp.zeros((slot_count, query_len), jnp.float32),
        jnp.zeros((query_len, slot_count, HD), jnp.float32),
    )
    key_piece = select_rows(lax.all_gather(key_pick, "seq", axis=0, tiled=True))
    value_piece = select_rows(lax.all_gather(value_pick, "seq", axis=0, tiled=True))
    piece_len = key_piece.shape[0]
    key_pos = jnp.arange(piece_len, dtype=jnp.int32)
    allowed = block_mask(query_blocks, key_pos // BLK, vertical_sel, slash_sel, query_pos, key_pos)
    max_parts = []
    total_parts = []
    sum_parts = []
    for lead in range(0, slot_count, 2):
        previous = (
            initial[0][lead : lead + 2],
            initial[1][lead : lead + 2],
            initial[2][:, lead : lead + 2],
        )
        updated = attend(
            previous,
            query_sel[:, lead : lead + 2],
            key_piece[:, lead : lead + 2],
            value_piece[:, lead : lead + 2],
            allowed[lead : lead + 2],
            score_scale,
        )
        max_parts.append(updated[0])
        total_parts.append(updated[1])
        sum_parts.append(updated[2])
    output = (
        jnp.concatenate(sum_parts, axis=1)
        / jnp.transpose(jnp.concatenate(total_parts, axis=0))[:, :, None]
    )
    return output.reshape(query_len, slot_count * HD).astype(jnp.bfloat16)


def solution(mesh):
    in_specs = (P("seq", "head"), P("seq", None), P("seq", None), P(), P(), P())
    out_specs = P("seq", "head")
    return jax.shard_map(
        per_device, mesh=mesh, in_specs=in_specs, out_specs=out_specs, check_vma=False
    )
```

profile of v0, /device:TPU:16, one launch (start us, length us, event | category | flops | bytes accessed | tf_op | source)
XLA Modules:
  0.0 250.0 jit_solution(17985091205724103392)
XLA Ops:
  6.5 0.0 copy-start
  6.5 0.0 all-gather.6.cloned.1.call-start
  6.5 0.7 all-gather.6.cloned.1.call-update
  7.3 0.0 all-gather.4.cloned.1.call-start
  7.3 0.7 compare_and_fusion
  8.1 0.0 copy-done
  8.1 0.6 gather_fusion.5
  8.7 0.9 copy_bitcast_fusion.1
  9.6 0.6 gather_fusion.1
  10.2 0.1 select_bitcast_fusion.3
  10.3 0.6 copy.48
  10.9 0.0 all-gather.4.cloned.1.call-update
  10.9 0.0 all-gather.8.cloned.1.call-start
  11.0 0.6 copy.49
  11.6 0.0 all-gather.8.cloned.1.call-update
  11.7 0.8 copy.28
  12.4 0.8 copy.29
  13.2 0.6 gather_fusion.3
  13.8 0.6 gather_fusion.4
  14.4 0.1 broadcast_select_fusion.4
  14.5 0.3 slice_reduce_fusion.7
  14.8 0.2 compare_reduce_fusion
  14.9 0.1 iota_compare_fusion
  15.1 0.1 broadcast_subtract_fusion
  15.2 2.2 or_and_fusion
  17.4 38.6 %all-gather.6.cloned.1.call-done = bf16[64,8192]{1,0:T(8,128)(2,1)} async-done(((bf16[64,512]{1,0:T(8,128)(2,1)}), bf16[64,8192]{1,0:T(8,128)(2,1)}) %all-gather.6.cloned.1.call-update) | async-done | bytes 1048592 | tf_op jit(solution)/shard_map/all_gather | solution.py:58
  56.0 1.5 copy_bitcast_fusion
  57.5 0.6 gather_fusion
  58.1 82.0 %all-gather.4.cloned.1.call-done = bf16[2048,512]{1,0:T(8,128)(2,1)} async-done(((bf16[64,512]{1,0:T(8,128)(2,1)}), bf16[2048,512]{1,0:T(8,128)(2,1)}) %all-gather.4.cloned.1.call-update) | async-done | bytes 2097168 | tf_op jit(solution)/shard_map/all_gather | solution.py:75
  140.1 3.9 %copy.26 = bf16[2048,512]{0,1:T(8,128)(2,1)} copy(bf16[2048,512]{1,0:T(8,128)(2,1)} %all-gather.4.cloned.1.call-done) | data formatting | bytes 4194304 | tf_op jit(solution)/shard_map/all_gather | solution.py:75
  144.1 3.0 %copy.27 = bf16[2048,4,128]{2,0,1:T(8,128)(2,1)S(1)} copy(bf16[2048,4,128]{0,2,1:T(8,128)(2,1)} %bitcast.53) | data formatting | bytes 4194304 | tf_op jit(solution)/shard_map/reshape | solution.py:67
  147.1 76.9 %all-gather.8.cloned.1.call-done = bf16[2048,512]{1,0:T(8,128)(2,1)} async-done(((bf16[64,512]{1,0:T(8,128)(2,1)}), bf16[2048,512]{1,0:T(8,128)(2,1)}) %all-gather.8.cloned.1.call-update) | async-done | bytes 2097168 | tf_op jit(solution)/shard_map/all_gather | solution.py:74
  224.1 4.0 %copy.33 = bf16[2048,512]{0,1:T(8,128)(2,1)} copy(bf16[2048,512]{1,0:T(8,128)(2,1)} %all-gather.8.cloned.1.call-done) | data formatting | bytes 4194304 | tf_op jit(solution)/shard_map/all_gather | solution.py:74
  228.0 4.0 %copy.34 = bf16[2048,4,128]{2,0,1:T(8,128)(2,1)} copy(bf16[2048,4,128]{0,2,1:T(8,128)(2,1)} %bitcast.54) | data formatting | bytes 4194304 | tf_op jit(solution)/shard_map/reshape | solution.py:67
  232.0 2.1 gather_fusion.2
  234.1 0.0 copy-start.1
  234.1 3.9 %gather_fusion.6 = bf16[4,2048,128]{2,1,0:T(8,128)(2,1)} fusion(bf16[2048,4,128]{2,0,1:T(8,128)(2,1)} %copy.34, s32[1024]{0:T(1024)S(1)} %pad_clamp_fusion), kind=kCustom, calls=%fused_computation.4.clone | custom fusion | bytes 4194320 | tf_op jit(solution)/shard_map/jit(_take)/gather | solution.py:67
  238.0 0.0 copy-done.1
  238.0 2.0 select_bitcast_fusion.1
  240.0 0.6 fusion.23
  240.7 0.7 fusion.24
  241.3 0.3 fusion.8
  241.6 0.4 convolution_bitcast_fusion
  242.0 0.4 convolution_bitcast_fusion.1
  242.4 0.3 fusion.6
  242.8 0.7 copy_bitcast_fusion.3
  (11 shorter events, 0.1 us)
Async XLA Ops:
  6.5 1.5 copy-start
  6.5 49.5 %all-gather.6.cloned.1.call-start = ((), (), s32[]{:S(2)}) async-start(), calls=%async_computation.1 | async-start | bytes 1114112 | tf_op jit(solution)/shard_map/all_gather | solution.py:58
  7.3 132.9 %all-gather.4.cloned.1.call-start = ((), (), s32[]{:S(2)}) async-start(), calls=%async_computation | async-start | bytes 2162688 | tf_op jit(solution)/shard_map/all_gather | solution.py:75
  10.9 213.1 %all-gather.8.cloned.1.call-start = ((), (), s32[]{:S(2)}) async-start(), calls=%async_computation.2 | async-start | bytes 2162688 | tf_op jit(solution)/shard_map/all_gather | solution.py:74
  234.1 3.9 %copy-start.1 = (bf16[4,2048,128]{2,1,0:T(8,128)(2,1)S(1)}, bf16[4,2048,128]{2,1,0:T(8,128)(2,1)}, u32[]{:S(2)}) copy-start(bf16[4,2048,128]{2,1,0:T(8,128)(2,1)} %gather_fusion.2) | copy-start | bytes 6291460
Sparse Core Ops, SparseCore 0:
  9.5 46.4 all-gather.5
  59.2 80.8 all-gather.3
  143.3 80.7 all-gather.7
where the time goes:
time: 251 us; the launch traced here: 250 us
  waiting for transfers between devices  198 us (79%)
  local copies, waits for them, and re-layouts  29.3 us (12%)
  between operations  13.3 us (5%)
  other arithmetic  6.95 us (3%)
    all_gather x1, waiting for transfers between devices, per_device(): lax.all_gather(value_pick, 'seq', axis=0, tiled=True)  82 us
    all_gather x1, waiting for transfers between devices, per_device(): key_piece = select_rows(lax.all_gather(key_pick, 'seq', axis=0, tiled=True))  76.9 us
    all_gather x1, waiting for transfers between devices, per_device(): gathered = lax.all_gather(queries, 'head', axis=1, tiled=True)  38.6 us
    reshape x2, local copies, waits for them, and re-layouts, select_rows(): rows.reshape(rows.shape[0], slot_count, HD)  6.99 us
    gather x2, local copies, waits for them, and re-layouts, select_rows(): jnp.take(rows.reshape(rows.shape[0], slot_count, HD), slot_column, axis=1)  5.99 us
  transfers between devices with their start and end apart: 3, of which 3 were waited for; matrix products, arithmetic and copies ran while one was open for 8% of the time, Pallas kernels for 0%

commit v1 on v0

v1 whole, which is shorter than its diff:
```python
import functools

import jax
import jax.numpy as jnp
from jax import lax
from jax.experimental import pallas as pl
from jax.experimental.pallas import tpu as pltpu
from jax.sharding import PartitionSpec as P

HD = 128
BLK = 64
HALF = BLK // 2
NX = 4
GROUP = 8
OWN = 4
LOW = -1e30
SCALE2 = (HD**-0.5) * 1.4426950408889634
MESH = pl.DeviceIdType.MESH


def kernel(
    ny, nx, nz,
    plan, vertical, slash, queries, keys, values, out,
    kvb, qb, qs, vt, scores, weights, bias, peak, part, got, gath, pick, rest,
    in_sem, y_send, x_send, kv_recv, q_sem, part_sem, z_send, z_recv, rest_sem,
):
    s = lax.axis_index("seq")
    h = lax.axis_index("head")
    y, x = s // nx, s % nx
    z, core = h // 2, h % 2
    sib = z * 2 + (1 - core)
    rows = GROUP * BLK

    kvb[...] = jnp.zeros_like(kvb)
    column = pl.ds(pl.multiple_of(z * HD, HD), HD)
    half = pl.ds(pl.multiple_of(core * HALF, HALF), HALF)
    loads = [
        pltpu.make_async_copy(keys.at[half, column], kvb.at[s, 0], in_sem.at[0]),
        pltpu.make_async_copy(values.at[half, column], kvb.at[s, 1], in_sem.at[1]),
        pltpu.make_async_copy(queries, qb.at[core], in_sem.at[2]),
    ]
    for load in loads:
        load.start()

    barrier = pltpu.get_barrier_semaphore()
    partners = [((y + t) % ny * nx + x, h) for t in range(1, ny)]
    partners += [(y * nx + (x + t) % nx, h) for t in range(1, nx)]
    partners += [(s, sib)]
    partners += [(s, (z + 1) % nz * 2 + core)]
    if nz > 2:
        partners += [(s, (z + nz - 1) % nz * 2 + core)]
    for partner in partners:
        pl.semaphore_signal(barrier, inc=1, device_id=partner, device_id_type=MESH)
    pl.semaphore_wait(barrier, len(partners))

    for load in loads:
        load.wait()

    def y_copy(t):
        return pltpu.make_async_remote_copy(
            src_ref=kvb.at[s], dst_ref=kvb.at[s], send_sem=y_send.at[t - 1], recv_sem=kv_recv.at[s],
            device_id=((y + t) * nx + x, h), device_id_type=MESH)

    def x_copy(row, t):
        b = row * nx + x
        return pltpu.make_async_remote_copy(
            src_ref=kvb.at[b], dst_ref=kvb.at[b], send_sem=x_send.at[row, t - 1], recv_sem=kv_recv.at[b],
            device_id=(y * nx + (x + t) % nx, h), device_id_type=MESH)

    def block_wait(b):
        pltpu.make_async_remote_copy(
            src_ref=kvb.at[b], dst_ref=kvb.at[b], send_sem=y_send.at[0], recv_sem=kv_recv.at[b],
            device_id=(s, sib), device_id_type=MESH).wait_recv()

    for t in range(1, ny):
        @pl.when(y + t < ny)
        def _():
            y_copy(t).start()
    for t in range(1, nx):
        x_copy(y, t).start()
    q_copy = pltpu.make_async_remote_copy(
        src_ref=qb.at[core], dst_ref=qb.at[core], send_sem=q_sem.at[0], recv_sem=q_sem.at[1],
        device_id=(s, sib), device_id_type=MESH)
    q_copy.start()

    head_rows = pl.ds(pl.multiple_of(z * GROUP, GROUP), GROUP)
    spread = (
        lax.broadcasted_iota(jnp.int32, (GROUP, rows), 0)
        == lax.broadcasted_iota(jnp.int32, (GROUP, rows), 1) // BLK
    ).astype(jnp.float32)

    def by_row(table):
        return lax.dot_general(
            table[head_rows, :].astype(jnp.float32), spread, (((0,), (0,)), ((), ())),
            preferred_element_type=jnp.float32)

    vert_rows = by_row(vertical)
    slash_rows = by_row(slash)
    blocks = lax.broadcasted_iota(jnp.int32, (ny * nx, rows), 0)
    block_f = blocks.astype(jnp.float32)
    gap_f = (s - blocks).astype(jnp.float32)
    hit = block_f < 0
    for n in range(vert_rows.shape[0]):
        hit = hit | (block_f == vert_rows[n : n + 1, :])
    for n in range(slash_rows.shape[0]):
        hit = hit | (gap_f == slash_rows[n : n + 1, :])
    bias[...] = jnp.where(hit & (blocks <= s), 0.0, LOW)

    for t in range(1, ny):
        @pl.when(y - t >= 0)
        def _():
            row = y - t
            block_wait(row * nx + x)
            for u in range(1, nx):
                x_copy(row, u).start()

    q_copy.wait()
    for i in range(GROUP):
        qs[i * BLK : (i + 1) * BLK, :] = qb[i // OWN, :, (i % OWN) * HD : (i % OWN + 1) * HD]

    peak[...] = jnp.full_like(peak, LOW)
    chunk = nx * HALF
    for row in range(ny):
        at = slice(row * chunk, (row + 1) * chunk)

        @pl.when(row <= y)
        def _():
            for u in range(1, nx):
                block_wait(row * nx + (x + u) % nx)
            k_rows = kvb[row * nx : (row + 1) * nx, 0].reshape(chunk, HD)
            v_rows = kvb[row * nx : (row + 1) * nx, 1].reshape(chunk, HD)
            vt[:, at] = v_rows.astype(jnp.float32).T.astype(jnp.bfloat16)
            raw = lax.dot_general(
                k_rows, qs[...], (((1,), (1,)), ((), ())), preferred_element_type=jnp.float32)
            raw = raw.reshape(nx, HALF, rows) + bias[row * nx : (row + 1) * nx, :].reshape(nx, 1, rows)
            shape = (nx, HALF, rows)
            key_at = (
                (row * nx + lax.broadcasted_iota(jnp.int32, shape, 0)) * BLK
                + core * HALF + lax.broadcasted_iota(jnp.int32, shape, 1))
            query_at = s * BLK + lax.broadcasted_iota(jnp.int32, shape, 2) % BLK
            raw = jnp.where(key_at <= query_at, raw, LOW).reshape(chunk, rows)
            scores[at, :] = raw
            peak[...] = jnp.maximum(peak[...], jnp.max(raw.reshape(chunk // 8, 8, rows), axis=0))

        @pl.when(row > y)
        def _():
            vt[:, at] = jnp.zeros((HD, chunk), jnp.bfloat16)
            weights[at, :] = jnp.zeros((chunk, rows), jnp.bfloat16)

    top = jnp.max(peak[...], axis=0, keepdims=True)
    peak[...] = jnp.zeros_like(peak)
    for row in range(ny):
        at = slice(row * chunk, (row + 1) * chunk)

        @pl.when(row <= y)
        def _():
            w = jnp.exp2((scores[at, :] - top) * SCALE2)
            peak[...] += jnp.sum(w.reshape(chunk // 8, 8, rows), axis=0)
            weights[at, :] = w.astype(jnp.bfloat16)

    total = jnp.sum(peak[...], axis=0, keepdims=True)
    sums = lax.dot_general(
        vt[...], weights[...], (((1,), (0,)), ((), ())), preferred_element_type=jnp.float32)
    mine = OWN * BLK
    for c in range(2):
        lanes = slice(c * mine, (c + 1) * mine)
        part[c, :HD, :] = sums[:, lanes]
        part[c, HD : HD + 8, :] = jnp.broadcast_to(top[:, lanes], (8, mine))
        part[c, HD + 8 :, :] = jnp.broadcast_to(total[:, lanes], (8, mine))
    part_copy = pltpu.make_async_remote_copy(
        src_ref=part.at[1 - core], dst_ref=got, send_sem=part_sem.at[0], recv_sem=part_sem.at[1],
        device_id=(s, sib), device_id_type=MESH)
    part_copy.start()
    part_copy.wait_recv()
    top_a, top_b = part[core, HD : HD + 1, :], got[HD : HD + 1, :]
    both = jnp.maximum(top_a, top_b)
    scale_a = jnp.exp2((top_a - both) * SCALE2)
    scale_b = jnp.exp2((top_b - both) * SCALE2)
    under = part[core, HD + 8 : HD + 9, :] * scale_a + got[HD + 8 : HD + 9, :] * scale_b
    mixed = (part[core, :HD, :] * scale_a + got[:HD, :] * scale_b) / under
    gath[z] = mixed.T.astype(jnp.bfloat16).reshape(OWN, BLK, HD)

    far = nz // 2
    pieces = [(0, 0, far), (0, 1, far - 1), (1, 1, far), (1, 0, far - 1)]

    def z_copy(way, piece, hop):
        step = 1 if way == 0 else nz - 1
        owner = (z + (nz - 1 if way == 0 else 1) * (hop - 1)) % nz
        block = gath.at[owner, pl.ds(piece * 2, 2)]
        return pltpu.make_async_remote_copy(
            src_ref=block, dst_ref=block, send_sem=z_send.at[way, piece, hop - 1],
            recv_sem=z_recv.at[way, piece, hop - 1],
            device_id=(s, (z + step) % nz * 2 + core), device_id_type=MESH)

    def z_wait(way, piece, hop):
        owner = (z + (nz - 1 if way == 0 else 1) * hop) % nz
        block = gath.at[owner, pl.ds(piece * 2, 2)]
        pltpu.make_async_remote_copy(
            src_ref=block, dst_ref=block, send_sem=z_send.at[way, piece, hop - 1],
            recv_sem=z_recv.at[way, piece, hop - 1],
            device_id=(s, sib), device_id_type=MESH).wait_recv()

    for hop in range(1, far + 1):
        for way, piece, hops in pieces:
            if hop <= hops:
                if hop > 1:
                    z_wait(way, piece, hop - 1)
                z_copy(way, piece, hop).start()
    for way, piece, hops in pieces:
        if hops:
            z_wait(way, piece, hops)

    for t in range(OWN):
        head = plan[sib * OWN + t]
        pick[t] = gath[head // GROUP, head % OWN]
    rest_copy = pltpu.make_async_remote_copy(
        src_ref=pick, dst_ref=rest, send_sem=rest_sem.at[0], recv_sem=rest_sem.at[1],
        device_id=(s, sib), device_id_type=MESH)
    rest_copy.start()
    rest_copy.wait_recv()
    for t in range(OWN):
        head = plan[h * OWN + t]
        here = (head // OWN) % 2 == core
        out[:, t * HD : (t + 1) * HD] = jnp.where(here, gath[head // GROUP, head % OWN], rest[t])

    for t in range(1, ny):
        @pl.when(y + t < ny)
        def _():
            y_copy(t).wait_send()
    for row in range(ny):
        @pl.when(row <= y)
        def _():
            for u in range(1, nx):
                x_copy(row, u).wait_send()
    part_copy.wait_send()
    for way, piece, hops in pieces:
        for hop in range(1, hops + 1):
            z_copy(way, piece, hop).wait_send()
    rest_copy.wait_send()


def per_device(nx, queries, keys, values, vertical, slash, plan):
    nz = lax.axis_size("head") // 2
    ny = lax.axis_size("seq") // nx
    nb = ny * nx
    rows = GROUP * BLK
    mine = OWN * BLK
    half_keys = nb * HALF
    far = nz // 2
    bf, f32 = jnp.bfloat16, jnp.float32
    vmem = pl.BlockSpec(memory_space=pltpu.VMEM)
    smem = pl.BlockSpec(memory_space=pltpu.SMEM)
    anywhere = pl.BlockSpec(memory_space=pl.ANY)
    dma = pltpu.SemaphoreType.DMA
    return pl.pallas_call(
        functools.partial(kernel, ny, nx, nz),
        out_shape=jax.ShapeDtypeStruct((BLK, OWN * HD), bf),
        in_specs=[smem, vmem, vmem, anywhere, anywhere, anywhere],
        out_specs=vmem,
        scratch_shapes=[
            pltpu.VMEM((nb, 2, HALF, HD), bf),
            pltpu.VMEM((2, BLK, OWN * HD), bf),
            pltpu.VMEM((rows, HD), bf),
            pltpu.VMEM((HD, half_keys), bf),
            pltpu.VMEM((half_keys, rows), f32),
            pltpu.VMEM((half_keys, rows), bf),
            pltpu.VMEM((nb, rows), f32),
            pltpu.VMEM((8, rows), f32),
            pltpu.VMEM((2, HD + 16, mine), f32),
            pltpu.VMEM((HD + 16, mine), f32),
            pltpu.VMEM((nz, OWN, BLK, HD), bf),
            pltpu.VMEM((OWN, BLK, HD), bf),
            pltpu.VMEM((OWN, BLK, HD), bf),
            dma((3,)),
            dma((ny,)),
            dma((ny, nx)),
            dma((nb,)),
            dma((2,)),
            dma((2,)),
            dma((2, 2, far)),
            dma((2, 2, far)),
            dma((2,)),
        ],
        compiler_params=pltpu.CompilerParams(
            collective_id=0, has_side_effects=True, vmem_limit_bytes=32 * 2**20),
    )(plan, vertical, slash, queries, keys, values)


def solution(mesh, nx=NX):
    in_specs = (P("seq", "head"), P("seq", None), P("seq", None), P(), P(), P())
    return jax.shard_map(
        functools.partial(per_device, nx), mesh=mesh, in_specs=in_specs,
        out_specs=P("seq", "head"), check_vma=False)
```

time: 251 us -> 44.6 us (0.18)
  the two profiles are of different devices: /device:TPU:16 before, /device:TPU:57 now
where the time goes in v1:
time: 44.6 us; the launch traced here: 44.4 us
  Pallas kernels  40.5 us (91%)
  local copies, waits for them, and re-layouts  3.9 us (9%)
    pallas_call x1, Pallas kernels, per_device(): pl.pallas_call(functools.partial(kernel, ny, nx, nz), out_shape=jax.Shape...  40.5 us
    unnamed x13, local copies, waits for them, and re-layouts  3.9 us

profile of v1, /device:TPU:57, one launch (start us, length us, event | category | flops | bytes accessed | tf_op | source)
XLA Modules:
  0.0 44.4 jit_solution(9077947991616124254)
XLA Ops:
  0.0 0.0 copy-start.4
  0.0 0.0 copy-start.2
  0.0 0.8 %copy.7.vertical = s32[64,8]{1,0:T(8,128)S(1)} copy(s32[64,8]{0,1:T(8,128)} %param.9) | data formatting | bytes 4096 | tf_op args[3]
  0.8 0.0 copy-done.4
  0.8 0.0 copy-start.3
  0.8 0.1 copy.8.slash
  0.9 0.0 copy-done.2
  0.9 0.6 %copy-done.3 = s32[64]{0:T(128)S(1)} copy-done((s32[64]{0:T(128)S(1)}, s32[64]{0:T(128)}, u32[]{:S(2)}) %copy-start.3) | copy-done | bytes 280
  1.5 0.0 copy-start
  1.5 0.9 %copy-done = bf16[64,1024]{1,0:T(8,128)(2,1)S(1)} copy-done((bf16[64,1024]{1,0:T(8,128)(2,1)S(1)}, bf16[64,1024]{1,0:T(8,128)(2,1)}, u32[]{:S(2)}) %copy-start) | copy-done | bytes 131096
  2.4 0.0 copy-start.1
  2.4 0.9 %copy-done.1 = bf16[64,1024]{1,0:T(8,128)(2,1)S(1)} copy-done((bf16[64,1024]{1,0:T(8,128)(2,1)S(1)}, bf16[64,1024]{1,0:T(8,128)(2,1)}, u32[]{:S(2)}) %copy-start.1) | copy-done | bytes 131096
  3.3 40.5 %shard_map.64 = bf16[64,512]{1,0:T(8,128)(2,1)S(1)} custom-call(s32[64]{0:T(128)S(1)} %copy-done.3, s32[64,8]{1,0:T(8,128)S(1)} %copy.7.vertical, s32[64,8]{1,0:T(8,128)S(1)} %copy.8.slash, bf16[64,512]{1,0:T(8,128)(2,1)S(1)} %copy-done.2, bf16[64,1024]{1,0:T(8,128)(2,1)S(1)} %copy-done, bf16[64,1024]{1,0:T(8,128)(2,1)S(1)} %copy-done.1), custom_call_target="tpu_custom_call" | custom-call | tf_op jit(solution)/shard_map/pallas_call | solution.py:255
  43.8 0.6 %copy.10 = bf16[64,512]{1,0:T(8,128)(2,1)} copy(bf16[64,512]{1,0:T(8,128)(2,1)S(1)} %shard_map.64) | data formatting | bytes 131072
Async XLA Ops:
  0.0 0.8 %copy-start.4 = (s32[64,8]{0,1:T(8,128)S(1)}, s32[64,8]{0,1:T(8,128)}, u32[]{:S(2)}) copy-start(s32[64,8]{0,1:T(8,128)} %param.10) | copy-start | bytes 6148
  0.0 0.9 %copy-start.2 = (bf16[64,512]{1,0:T(8,128)(2,1)S(1)}, bf16[64,512]{1,0:T(8,128)(2,1)}, u32[]{:S(2)}) copy-start(bf16[64,512]{1,0:T(8,128)(2,1)} %queries.1) | copy-start | bytes 196612
  0.8 0.7 %copy-start.3 = (s32[64]{0:T(128)S(1)}, s32[64]{0:T(128)}, u32[]{:S(2)}) copy-start(s32[64]{0:T(128)} %plan.1) | copy-start | bytes 772
  1.5 0.9 %copy-start = (bf16[64,1024]{1,0:T(8,128)(2,1)S(1)}, bf16[64,1024]{1,0:T(8,128)(2,1)}, u32[]{:S(2)}) copy-start(bf16[64,1024]{1,0:T(8,128)(2,1)} %keys.1) | copy-start | bytes 393220
  2.4 0.9 %copy-start.1 = (bf16[64,1024]{1,0:T(8,128)(2,1)S(1)}, bf16[64,1024]{1,0:T(8,128)(2,1)}, u32[]{:S(2)}) copy-start(bf16[64,1024]{1,0:T(8,128)(2,1)} %values.1) | copy-start | bytes 393220

commit v2 on v1

v2 whole, which is shorter than its diff:
```python
import functools

import jax
import jax.numpy as jnp
from jax import lax
from jax.experimental import pallas as pl
from jax.experimental.pallas import tpu as pltpu
from jax.sharding import PartitionSpec as P

HD = 128
BLK = 64
HALF = BLK // 2
NX = 4
GROUP = 8
OWN = 4
LOW = -1e30
SCALE2 = (HD**-0.5) * 1.4426950408889634
MESH = pl.DeviceIdType.MESH


def kernel(
    ny, nx, nz,
    plan_hbm, vertical_hbm, slash_hbm, queries, keys, values, out,
    plan, vertical, slash, kvb, qb, qs, bias, top, total, part, got, gath, pick, rest,
    in_sem, y_send, far_send, across_send, x_send, kv_recv, q_sem, part_sem, z_send, pass_send, z_recv, rest_sem, late,
):
    s = lax.axis_index("seq")
    h = lax.axis_index("head")
    y, x = s // nx, s % nx
    z, core = h // 2, h % 2
    sib = z * 2 + (1 - core)
    ne = nz // 2
    early = z < ne
    rows = GROUP * BLK
    mine = OWN * BLK
    chunk = nx * HALF
    sides = [t for t in sorted({1, nx - 1}) if t % nx]
    across = nx // 2 if nx > 2 else 0

    def signal(where, device):
        pl.semaphore_signal(where, inc=1, device_id=device, device_id_type=MESH)

    def remote(src, dst, send, recv, device):
        return pltpu.make_async_remote_copy(
            src_ref=src, dst_ref=dst, send_sem=send, recv_sem=recv, device_id=device, device_id_type=MESH)

    column = pl.ds(pl.multiple_of(z * HD, HD), HD)
    half = pl.ds(pl.multiple_of(core * HALF, HALF), HALF)
    k_load = pltpu.make_async_copy(keys.at[half, column], kvb.at[s, 0], in_sem.at[0])
    v_load = pltpu.make_async_copy(values.at[half, column], kvb.at[s, 1], in_sem.at[1])
    q_load = pltpu.make_async_copy(queries, qb.at[core], in_sem.at[2])
    plan_load = pltpu.make_async_copy(plan_hbm, plan, in_sem.at[3])
    vert_load = pltpu.make_async_copy(vertical_hbm, vertical, in_sem.at[4])
    slash_load = pltpu.make_async_copy(slash_hbm, slash, in_sem.at[5])
    loads = [k_load, v_load, q_load, vert_load, slash_load, plan_load]
    for load in loads:
        load.start()

    barrier = pltpu.get_barrier_semaphore()
    partners = [((y + t) % ny * nx + x, h) for t in range(1, ny)]
    partners += [(y * nx + (x + t) % nx, h) for t in range(1, nx)]
    partners += [(s, sib)]
    for partner in partners:
        signal(barrier, partner)
    for other in range(1, nz):
        @pl.when(other > z)
        def _():
            signal(barrier, (s, other * 2 + core))
    pl.semaphore_wait(barrier, len(partners) + z)

    def y_copy(t):
        return remote(kvb.at[s], kvb.at[s], y_send.at[t - 1], kv_recv.at[s], ((y + t) * nx + x, h))

    over = y * nx + (x + across) % nx

    def far_copy(t):
        return remote(kvb.at[over], kvb.at[over], far_send.at[t - 1], kv_recv.at[over], ((y + t) * nx + x, h))

    across_copy = remote(kvb.at[s], kvb.at[s], across_send.at[0], kv_recv.at[s], (over, h))

    def x_copy(row, side):
        b = row * nx + x
        to = (x + sides[side]) % nx
        return remote(kvb.at[b], kvb.at[b], x_send.at[row, side], kv_recv.at[b], (y * nx + to, h))

    def block_wait(b):
        remote(kvb.at[b], kvb.at[b], y_send.at[0], kv_recv.at[b], (s, sib)).wait_recv()

    def above(t, action):
        @pl.when(y + t < ny)
        def _():
            action(t)

    k_load.wait()
    v_load.wait()
    if across:
        across_copy.start()
    for t in reversed(range(1, ny)):
        above(t, lambda t: y_copy(t).start())
    for side in range(len(sides)):
        x_copy(y, side).start()
    q_load.wait()
    q_copy = remote(qb.at[core], qb.at[core], q_sem.at[0], q_sem.at[1], (s, sib))
    q_copy.start()
    for other in range(nz - 1):
        @pl.when(other < z)
        def _():
            signal(late.at[z], (s, other * 2 + core))

    vert_load.wait()
    slash_load.wait()
    heads = vertical.shape[1]
    spread = (
        lax.broadcasted_iota(jnp.int32, (heads, rows), 0)
        == z * GROUP + lax.broadcasted_iota(jnp.int32, (heads, rows), 1) // BLK
    ).astype(jnp.float32)

    def by_row(table):
        return jnp.dot(table[...].astype(jnp.float32), spread, preferred_element_type=jnp.float32)

    vert_rows = by_row(vertical)
    slash_rows = by_row(slash)
    blocks = lax.broadcasted_iota(jnp.int32, (ny * nx, rows), 0)
    block_f = blocks.astype(jnp.float32)
    gap_f = (s - blocks).astype(jnp.float32)
    hit = block_f < 0
    for n in range(vert_rows.shape[0]):
        hit = hit | (block_f == vert_rows[n : n + 1, :])
    for n in range(slash_rows.shape[0]):
        hit = hit | (gap_f == slash_rows[n : n + 1, :])
    bias[...] = jnp.where(hit & (blocks <= s), 0.0, LOW).reshape(ny, nx, 1, rows)
    top[...] = jnp.full_like(top, LOW)
    total[...] = jnp.zeros_like(total)
    part[...] = jnp.zeros_like(part)

    nearest = sorted(range(1, ny), key=lambda t: min(t, ny - t))
    if across:
        block_wait(over)
        for t in reversed(range(1, ny)):
            above(t, lambda t: far_copy(t).start())
    for t in nearest:
        @pl.when(y - t >= 0)
        def _():
            block_wait((y - t) * nx + x)
            for side in range(len(sides)):
                x_copy(y - t, side).start()

    q_copy.wait()
    for i in range(GROUP):
        qs[i * BLK : (i + 1) * BLK, :] = qb[i // OWN, :, (i % OWN) * HD : (i % OWN + 1) * HD]

    def attend(row):
        these = pl.ds(row * nx, nx)
        k_rows = kvb[these, 0].reshape(chunk, HD)
        v_rows = kvb[these, 1].reshape(chunk, HD)
        v_turned = v_rows.astype(jnp.float32).T.astype(jnp.bfloat16)
        raw = lax.dot_general(
            k_rows, qs[...], (((1,), (1,)), ((), ())), preferred_element_type=jnp.float32)
        shape = (nx, HALF, rows)
        raw = raw.reshape(shape) + bias[row]
        key_at = (
            (row * nx + lax.broadcasted_iota(jnp.int32, shape, 0)) * BLK
            + core * HALF + lax.broadcasted_iota(jnp.int32, shape, 1))
        query_at = s * BLK + lax.broadcasted_iota(jnp.int32, shape, 2) % BLK
        raw = jnp.where(key_at <= query_at, raw, LOW).reshape(chunk, rows)
        old = top[...]
        new = jnp.maximum(old, jnp.max(raw, axis=0, keepdims=True))
        w = jnp.exp2((raw - new) * SCALE2)
        keep = jnp.exp2((old - new) * SCALE2)
        top[...] = new
        total[...] = total[...] * keep + jnp.sum(w, axis=0, keepdims=True)
        more = jnp.dot(v_turned, w.astype(jnp.bfloat16), preferred_element_type=jnp.float32)
        for c in range(2):
            lanes = slice(c * mine, (c + 1) * mine)
            part[c, :HD, :] = part[c, :HD, :] * keep[:, lanes] + more[:, lanes]

    def one_row(row):
        for u in sides:
            block_wait(row * nx + (x + u) % nx)
        if across:
            @pl.when(row < y)
            def _():
                block_wait(row * nx + (x + across) % nx)
        attend(row)

    one_row(y)
    for t in nearest:
        @pl.when(y - t >= 0)
        def _():
            one_row(y - t)

    for c in range(2):
        lanes = slice(c * mine, (c + 1) * mine)
        part[c, HD : HD + 8, :] = jnp.broadcast_to(top[:, lanes], (8, mine))
        part[c, HD + 8 :, :] = jnp.broadcast_to(total[:, lanes], (8, mine))
    part_copy = remote(part.at[1 - core], got, part_sem.at[0], part_sem.at[1], (s, sib))
    part_copy.start()
    part_copy.wait_recv()
    top_a, top_b = part[core, HD : HD + 1, :], got[HD : HD + 1, :]
    both = jnp.maximum(top_a, top_b)
    scale_a = jnp.exp2((top_a - both) * SCALE2)
    scale_b = jnp.exp2((top_b - both) * SCALE2)
    under = part[core, HD + 8 : HD + 9, :] * scale_a + got[HD + 8 : HD + 9, :] * scale_b
    mixed = (part[core, :HD, :] * scale_a + got[:HD, :] * scale_b) / under
    gath[z] = mixed.T.astype(jnp.bfloat16).reshape(OWN, BLK, HD)

    top_edge, low_edge = nz - 1, ne
    edges = [sorted({0, ne - 1}), sorted({low_edge, top_edge})]
    passes = ne >= 4
    upper = range(nz - ne // 2, nz) if passes else []
    lower = [source for source in range(ne, nz) if source not in upper]

    def send(source, target, sem):
        return remote(gath.at[source], gath.at[source], sem, z_recv.at[source], (s, target * 2 + core))

    def z_copy(target):
        return send(z, target, z_send.at[target])

    def pass_copy(source, target, lane=0):
        return send(source, target, pass_send.at[lane, source])

    def late_wait(target):
        @pl.when(target > z)
        def _():
            pl.semaphore_wait(late.at[target], 1)

    def arrive(source):
        @pl.when(source != z)
        def _():
            pass_copy(source, 0).wait_recv()

    routes = []
    if passes:
        routes += [(0, source, 1, 0) for source in reversed(upper)]
        for source in lower:
            routes += [(ne - 1, source, ne - 2, 0), (ne - 1, source, 1, 1)]
        routes += [(ne - 1, source, ne - 2, 0) for source in upper]
        routes += [(top_edge, source, top_edge - 1, 0) for source in range(ne)]
        routes += [(low_edge, source, low_edge + 1, 0) for source in range(ne)]

    def relay(plane, order):
        @pl.when(z == plane)
        def _():
            for source in order:
                arrive(source)
                for by, of, target, lane in routes:
                    if by == plane and of == source:
                        pass_copy(source, target, lane).start()

    @pl.when(early)
    def _():
        for target in range(ne):
            late_wait(target)

            @pl.when(target != z)
            def _():
                z_copy(target).start()
        for target in reversed(range(ne, nz)):
            late_wait(target)
            if target in edges[1]:
                z_copy(target).start()
        for source in range(ne):
            arrive(source)
        relay(0, list(reversed(range(ne, nz))))
        for plane in range(1, ne):
            relay(plane, list(range(ne, nz)))

    @pl.when(jnp.logical_not(early))
    def _():
        high = z >= nz - ne // 2
        if len(edges[0]) == 2:
            first = jnp.where(high, 0, ne - 1)
            second = ne - 1 - first
            send(z, first, z_send.at[0]).start()
            send(z, second, z_send.at[1]).start()
        else:
            send(z, 0, z_send.at[0]).start()
        for target in range(ne, nz):
            late_wait(target)

            @pl.when(target != z)
            def _():
                z_copy(target).start()
        for plane in range(ne, nz):
            relay(plane, list(range(ne)))
        for source in range(ne, nz):
            arrive(source)

    plan_load.wait()
    for t in range(OWN):
        head = plan[sib * OWN + t]
        pick[t] = gath[head // GROUP, head % OWN]
    rest_copy = remote(pick, rest, rest_sem.at[0], rest_sem.at[1], (s, sib))
    rest_copy.start()
    rest_copy.wait_recv()
    for t in range(OWN):
        head = plan[h * OWN + t]
        here = (head // OWN) % 2 == core
        out[:, t * HD : (t + 1) * HD] = jnp.where(here, gath[head // GROUP, head % OWN], rest[t])

    if across:
        across_copy.wait_send()
    for t in range(1, ny):
        above(t, lambda t: y_copy(t).wait_send())
        if across:
            above(t, lambda t: far_copy(t).wait_send())
    for row in range(ny):
        @pl.when(row <= y)
        def _():
            for side in range(len(sides)):
                x_copy(row, side).wait_send()
    part_copy.wait_send()

    @pl.when(early)
    def _():
        for target in range(ne):
            @pl.when(target != z)
            def _():
                z_copy(target).wait_send()
        for target in edges[1]:
            z_copy(target).wait_send()

    @pl.when(jnp.logical_not(early))
    def _():
        for target in range(len(edges[0])):
            z_copy(target).wait_send()
        for target in range(ne, nz):
            @pl.when(target != z)
            def _():
                z_copy(target).wait_send()
    for by, of, target, lane in routes:
        @pl.when(z == by)
        def _():
            pass_copy(of, target, lane).wait_send()
    rest_copy.wait_send()


def per_device(nx, queries, keys, values, vertical, slash, plan):
    nz = lax.axis_size("head") // 2
    ny = lax.axis_size("seq") // nx
    nb = ny * nx
    rows = GROUP * BLK
    mine = OWN * BLK
    bf, f32 = jnp.bfloat16, jnp.float32
    hbm = pl.BlockSpec(memory_space=pltpu.HBM)
    dma = pltpu.SemaphoreType.DMA
    tables = (vertical.shape[1], vertical.shape[0])
    return pl.pallas_call(
        functools.partial(kernel, ny, nx, nz),
        out_shape=jax.ShapeDtypeStruct((BLK, OWN * HD), bf),
        in_specs=[hbm] * 6,
        out_specs=pl.BlockSpec(memory_space=pltpu.VMEM),
        scratch_shapes=[
            pltpu.SMEM(plan.shape, jnp.int32),
            pltpu.VMEM(tables, jnp.int32),
            pltpu.VMEM(tables, jnp.int32),
            pltpu.VMEM((nb, 2, HALF, HD), bf),
            pltpu.VMEM((2, BLK, OWN * HD), bf),
            pltpu.VMEM((rows, HD), bf),
            pltpu.VMEM((ny, nx, 1, rows), f32),
            pltpu.VMEM((1, rows), f32),
            pltpu.VMEM((1, rows), f32),
            pltpu.VMEM((2, HD + 16, mine), f32),
            pltpu.VMEM((HD + 16, mine), f32),
            pltpu.VMEM((nz, OWN, BLK, HD), bf),
            pltpu.VMEM((OWN, BLK, HD), bf),
            pltpu.VMEM((OWN, BLK, HD), bf),
            dma((6,)),
            dma((ny,)),
            dma((ny,)),
            dma((1,)),
            dma((ny, 2)),
            dma((nb,)),
            dma((2,)),
            dma((2,)),
            dma((nz,)),
            dma((2, nz)),
            dma((nz,)),
            dma((2,)),
            pltpu.SemaphoreType.REGULAR((nz,)),
        ],
        compiler_params=pltpu.CompilerParams(
            collective_id=0, has_side_effects=True, vmem_limit_bytes=60 * 2**20),
    )(plan, vertical.T, slash.T, queries, keys, values)


def solution(mesh, nx=NX):
    in_specs = (P("seq", "head"), P("seq", None), P("seq", None), P(), P(), P())
    return jax.shard_map(
        functools.partial(per_device, nx), mesh=mesh, in_specs=in_specs,
        out_specs=P("seq", "head"), check_vma=False)
```

time: 44.6 us -> 41.3 us (0.926)
  the two profiles are of different devices: /device:TPU:57 before, /device:TPU:113 now
where the time goes in v2:
time: 41.3 us; the launch traced here: 41.1 us
  Pallas kernels  39.6 us (96%)
  local copies, waits for them, and re-layouts  1.47 us (4%)
    pallas_call x1, Pallas kernels, per_device(): pl.pallas_call(functools.partial(kernel, ny, nx, nz), out_shape=jax.Shape...  39.6 us
    unnamed x1, local copies, waits for them, and re-layouts  1.47 us

profile of v2, /device:TPU:113, one launch (start us, length us, event | category | flops | bytes accessed | tf_op | source)
XLA Modules:
  0.0 41.1 jit_solution(15422134402163409930)
XLA Ops:
  0.0 39.6 %shard_map.64 = bf16[64,512]{1,0:T(8,128)(2,1)} custom-call(s32[64]{0:T(128)} %plan_hbm.1, s32[8,64]{1,0:T(8,128)} %bitcast.2, s32[8,64]{1,0:T(8,128)} %bitcast.3, bf16[64,512]{1,0:T(8,128)(2,1)} %queries.1, bf16[64,1024]{1,0:T(8,128)(2,1)} %keys.1, bf16[64,1024]{1,0:T(8,128)(2,1)} %values.1), custom_call_target="tpu_custom_call" | custom-call | tf_op jit(solution)/shard_map/pallas_call | solution.py:348
  39.6 1.5 %copy.8 = bf16[64,512]{1,0:T(8,128)(2,1)} copy(bf16[64,512]{1,0:T(8,128)(2,1)} %shard_map.64) | data formatting | bytes 131072

commit v3 on v2

--- a/solution.py
+++ b/solution.py
@@ -20,8 +20,8 @@
 
 def kernel(
     ny, nx, nz,
-    plan_hbm, vertical_hbm, slash_hbm, queries, keys, values, out,
-    plan, vertical, slash, kvb, qb, qs, bias, top, total, part, got, gath, pick, rest,
+    plan_hbm, vertical_hbm, slash_hbm, queries, keys, values, out, rest,
+    plan, vertical, slash, kvb, qb, qs, bias, top, total, part, got, gath, pick, own,
     in_sem, y_send, far_send, across_send, x_send, kv_recv, q_sem, part_sem, z_send, pass_send, z_recv, rest_sem, late,
 ):
     s = lax.axis_index("seq")
@@ -57,16 +57,21 @@
         load.start()
 
     barrier = pltpu.get_barrier_semaphore()
-    partners = [((y + t) % ny * nx + x, h) for t in range(1, ny)]
-    partners += [(y * nx + (x + t) % nx, h) for t in range(1, nx)]
+    partners = [(y * nx + (x + t) % nx, h) for t in range(1, nx)]
     partners += [(s, sib)]
     for partner in partners:
         signal(barrier, partner)
+
+    def greet(row, carry):
+        signal(barrier, (row * nx + x, h))
+        return carry
+
+    lax.fori_loop(0, y, greet, 0)
     for other in range(1, nz):
         @pl.when(other > z)
         def _():
             signal(barrier, (s, other * 2 + core))
-    pl.semaphore_wait(barrier, len(partners) + z)
+    pl.semaphore_wait(barrier, len(partners) + ny - 1 - y + z)
 
     def y_copy(t):
         return remote(kvb.at[s], kvb.at[s], y_send.at[t - 1], kv_recv.at[s], ((y + t) * nx + x, h))
@@ -86,17 +91,30 @@
     def block_wait(b):
         remote(kvb.at[b], kvb.at[b], y_send.at[0], kv_recv.at[b], (s, sib)).wait_recv()
 
-    def above(t, action):
-        @pl.when(y + t < ny)
-        def _():
-            action(t)
+    def above(action):
+        def step(i, carry):
+            action(ny - 1 - y - i)
+            return carry
+
+        lax.fori_loop(0, ny - 1 - y, step, 0)
+
+    def below(action, first):
+        def step(i, carry):
+            t = jnp.where(i % 2 == 1, (i + 1) // 2, ny - i // 2) % ny
+
+            @pl.when(t <= y)
+            def _():
+                action(y - t)
+
+            return carry
+
+        lax.fori_loop(first, ny, step, 0)
 
     k_load.wait()
     v_load.wait()
     if across:
         across_copy.start()
-    for t in reversed(range(1, ny)):
-        above(t, lambda t: y_copy(t).start())
+    above(lambda t: y_copy(t).start())
     for side in range(len(sides)):
         x_copy(y, side).start()
     q_load.wait()
@@ -114,36 +132,39 @@
         lax.broadcasted_iota(jnp.int32, (heads, rows), 0)
         == z * GROUP + lax.broadcasted_iota(jnp.int32, (heads, rows), 1) // BLK
     ).astype(jnp.float32)
-
-    def by_row(table):
-        return jnp.dot(table[...].astype(jnp.float32), spread, preferred_element_type=jnp.float32)
-
-    vert_rows = by_row(vertical)
-    slash_rows = by_row(slash)
-    blocks = lax.broadcasted_iota(jnp.int32, (ny * nx, rows), 0)
-    block_f = blocks.astype(jnp.float32)
-    gap_f = (s - blocks).astype(jnp.float32)
-    hit = block_f < 0
-    for n in range(vert_rows.shape[0]):
-        hit = hit | (block_f == vert_rows[n : n + 1, :])
-    for n in range(slash_rows.shape[0]):
-        hit = hit | (gap_f == slash_rows[n : n + 1, :])
-    bias[...] = jnp.where(hit & (blocks <= s), 0.0, LOW).reshape(ny, nx, 1, rows)
+    blocks = lax.broadcasted_iota(jnp.int32, (ny * nx, heads), 0)
+    hit = blocks < 0
+    for n in range(vertical.shape[0]):
+        hit = hit | (blocks == vertical[n : n + 1, :])
+    for n in range(slash.shape[0]):
+        hit = hit | (s - blocks == slash[n : n + 1, :])
+    open_ = jnp.where(hit & (blocks <= s), 1.0, 0.0)
+    open_rows = jnp.dot(open_, spread, preferred_element_type=jnp.float32)
+    bias[...] = jnp.where(open_rows > 0.5, 0.0, LOW).reshape(ny, nx, 1, rows)
     top[...] = jnp.full_like(top, LOW)
     total[...] = jnp.zeros_like(total)
     part[...] = jnp.zeros_like(part)
 
-    nearest = sorted(range(1, ny), key=lambda t: min(t, ny - t))
     if across:
-        block_wait(over)
-        for t in reversed(range(1, ny)):
-            above(t, lambda t: far_copy(t).start())
-    for t in nearest:
-        @pl.when(y - t >= 0)
-        def _():
-            block_wait((y - t) * nx + x)
-            for side in range(len(sides)):
-                x_copy(y - t, side).start()
+        @pl.when(core == 0)
+        def _():
+            block_wait(over)
+            above(lambda t: far_copy(t).start())
+
+    def wide_copy(row):
+        b = row * nx + x
+        return remote(kvb.at[b], kvb.at[b], far_send.at[row], kv_recv.at[b], (over, h))
+
+    def forward(row):
+        block_wait(row * nx + x)
+        if across:
+            @pl.when(core == 1)
+            def _():
+                wide_copy(row).start()
+        for side in range(len(sides)):
+            x_copy(row, side).start()
+
+    below(forward, 1)
 
     q_copy.wait()
     for i in range(GROUP):
@@ -178,16 +199,12 @@
         for u in sides:
             block_wait(row * nx + (x + u) % nx)
         if across:
-            @pl.when(row < y)
+            @pl.when((row < y) | (core == 1))
             def _():
                 block_wait(row * nx + (x + across) % nx)
         attend(row)
 
-    one_row(y)
-    for t in nearest:
-        @pl.when(y - t >= 0)
-        def _():
-            one_row(y - t)
+    below(one_row, 0)
 
     for c in range(2):
         lanes = slice(c * mine, (c + 1) * mine)
@@ -231,10 +248,10 @@
 
     routes = []
     if passes:
-        routes += [(0, source, 1, 0) for source in reversed(upper)]
+        for source in upper:
+            routes += [(0, source, 1, 0), (0, source, ne - 2, 1)]
         for source in lower:
             routes += [(ne - 1, source, ne - 2, 0), (ne - 1, source, 1, 1)]
-        routes += [(ne - 1, source, ne - 2, 0) for source in upper]
         routes += [(top_edge, source, top_edge - 1, 0) for source in range(ne)]
         routes += [(low_edge, source, low_edge + 1, 0) for source in range(ne)]
 
@@ -272,43 +289,53 @@
             first = jnp.where(high, 0, ne - 1)
             second = ne - 1 - first
             send(z, first, z_send.at[0]).start()
+            for target in range(ne, nz):
+                late_wait(target)
+
+                @pl.when(target != z)
+                def _():
+                    z_copy(target).start()
+            z_copy(0).wait_send()
             send(z, second, z_send.at[1]).start()
         else:
             send(z, 0, z_send.at[0]).start()
-        for target in range(ne, nz):
-            late_wait(target)
-
-            @pl.when(target != z)
-            def _():
-                z_copy(target).start()
         for plane in range(ne, nz):
             relay(plane, list(range(ne)))
         for source in range(ne, nz):
             arrive(source)
 
     plan_load.wait()
-    for t in range(OWN):
-        head = plan[sib * OWN + t]
-        pick[t] = gath[head // GROUP, head % OWN]
+
+    def collect(into, device):
+        for t in range(OWN):
+            head = plan[device * OWN + t]
+            item = gath[head // GROUP, head % OWN]
+            into[:, t * HD : (t + 1) * HD] = jnp.where((head // OWN) % 2 == core, item, jnp.zeros_like(item))
+
+    collect(pick, sib)
     rest_copy = remote(pick, rest, rest_sem.at[0], rest_sem.at[1], (s, sib))
     rest_copy.start()
-    rest_copy.wait_recv()
-    for t in range(OWN):
-        head = plan[h * OWN + t]
-        here = (head // OWN) % 2 == core
-        out[:, t * HD : (t + 1) * HD] = jnp.where(here, gath[head // GROUP, head % OWN], rest[t])
+    collect(own, h)
+    own_copy = pltpu.make_async_copy(own, out, in_sem.at[0])
+    own_copy.start()
 
     if across:
         across_copy.wait_send()
-    for t in range(1, ny):
-        above(t, lambda t: y_copy(t).wait_send())
-        if across:
-            above(t, lambda t: far_copy(t).wait_send())
-    for row in range(ny):
-        @pl.when(row <= y)
-        def _():
-            for side in range(len(sides)):
-                x_copy(row, side).wait_send()
+    above(lambda t: y_copy(t).wait_send())
+    if across:
+        @pl.when(core == 0)
+        def _():
+            above(lambda t: far_copy(t).wait_send())
+
+        @pl.when(core == 1)
+        def _():
+            below(lambda row: wide_copy(row).wait_send(), 1)
+
+    def left(row):
+        for side in range(len(sides)):
+            x_copy(row, side).wait_send()
+
+    below(left, 0)
     part_copy.wait_send()
 
     @pl.when(early)
@@ -322,8 +349,7 @@
 
     @pl.when(jnp.logical_not(early))
     def _():
-        for target in range(len(edges[0])):
-            z_copy(target).wait_send()
+        z_copy(len(edges[0]) - 1).wait_send()
         for target in range(ne, nz):
             @pl.when(target != z)
             def _():
@@ -332,7 +358,8 @@
         @pl.when(z == by)
         def _():
             pass_copy(of, target, lane).wait_send()
-    rest_copy.wait_send()
+    rest_copy.wait()
+    own_copy.wait()
 
 
 def per_device(nx, queries, keys, values, vertical, slash, plan):
@@ -345,11 +372,11 @@
     hbm = pl.BlockSpec(memory_space=pltpu.HBM)
     dma = pltpu.SemaphoreType.DMA
     tables = (vertical.shape[1], vertical.shape[0])
-    return pl.pallas_call(
+    out, rest = pl.pallas_call(
         functools.partial(kernel, ny, nx, nz),
-        out_shape=jax.ShapeDtypeStruct((BLK, OWN * HD), bf),
+        out_shape=[jax.ShapeDtypeStruct((BLK, OWN * HD), bf)] * 2,
         in_specs=[hbm] * 6,
-        out_specs=pl.BlockSpec(memory_space=pltpu.VMEM),
+        out_specs=[hbm] * 2,
         scratch_shapes=[
             pltpu.SMEM(plan.shape, jnp.int32),
             pltpu.VMEM(tables, jnp.int32),
@@ -363,8 +390,8 @@
             pltpu.VMEM((2, HD + 16, mine), f32),
             pltpu.VMEM((HD + 16, mine), f32),
             pltpu.VMEM((nz, OWN, BLK, HD), bf),
-            pltpu.VMEM((OWN, BLK, HD), bf),
-            pltpu.VMEM((OWN, BLK, HD), bf),
+            pltpu.VMEM((BLK, OWN * HD), bf),
+            pltpu.VMEM((BLK, OWN * HD), bf),
             dma((6,)),
             dma((ny,)),
             dma((ny,)),
@@ -382,6 +409,7 @@
         compiler_params=pltpu.CompilerParams(
             collective_id=0, has_side_effects=True, vmem_limit_bytes=60 * 2**20),
     )(plan, vertical.T, slash.T, queries, keys, values)
+    return out + rest
 
 
 def solution(mesh, nx=NX):

time: 41.3 us -> 39.4 us (0.954)
  the two profiles are of different devices: /device:TPU:113 before, /device:TPU:57 now
where the time goes in v3:
time: 39.4 us; the launch traced here: 39.1 us
  Pallas kernels  37.6 us (95%)
  other arithmetic  1.52 us (4%)
    pallas_call x1, Pallas kernels, per_device(): pl.pallas_call(functools.partial(kernel, ny, nx, nz), out_shape=[jax.Shap...  37.6 us
    add x1, other arithmetic, per_device(): return out + rest  1.52 us

profile of v3, /device:TPU:57, one launch (start us, length us, event | category | flops | bytes accessed | tf_op | source)
XLA Modules:
  0.0 39.1 jit_solution(3090233931683279804)
XLA Ops:
  0.0 37.6 %shard_map.64 = (bf16[64,512]{1,0:T(8,128)(2,1)}, bf16[64,512]{1,0:T(8,128)(2,1)}) custom-call(s32[64]{0:T(128)} %plan_hbm.1, s32[8,64]{1,0:T(8,128)} %bitcast.2, s32[8,64]{1,0:T(8,128)} %bitcast.3, bf16[64,512]{1,0:T(8,128)(2,1)} %queries.1, bf16[64,1024]{1,0:T(8,128)(2,1)} %keys.1, bf16[64,1024]{1,0:T(8,128)(2,1)} %values.1), custom_call_target="tpu_custom_call" | custom-call | tf_op jit(solution)/shard_map/pallas_call | solution.py:375
  37.6 1.5 %add.3 = bf16[64,512]{1,0:T(8,128)(2,1)} add(bf16[64,512]{1,0:T(8,128)(2,1)} %get-tuple-element.7, bf16[64,512]{1,0:T(8,128)(2,1)} %get-tuple-element.8) | non-fusion elementwise | flops 32768 | bytes 196608 | tf_op jit(solution)/shard_map/add | solution.py:412

commit v4 on v3

--- a/solution.py
+++ b/solution.py
@@ -21,7 +21,7 @@
 def kernel(
     ny, nx, nz,
     plan_hbm, vertical_hbm, slash_hbm, queries, keys, values, out, rest,
-    plan, vertical, slash, kvb, qb, qs, bias, top, total, part, got, gath, pick, own,
+    plan, vertical, slash, kvb, qb, qs, bias, top, total, part, got, gath, pick,
     in_sem, y_send, far_send, across_send, x_send, kv_recv, q_sem, part_sem, z_send, pass_send, z_recv, rest_sem, late,
 ):
     s = lax.axis_index("seq")
@@ -170,7 +170,7 @@
     for i in range(GROUP):
         qs[i * BLK : (i + 1) * BLK, :] = qb[i // OWN, :, (i % OWN) * HD : (i % OWN + 1) * HD]
 
-    def attend(row):
+    def attend(row, diagonal):
         these = pl.ds(row * nx, nx)
         k_rows = kvb[these, 0].reshape(chunk, HD)
         v_rows = kvb[these, 1].reshape(chunk, HD)
@@ -179,11 +179,13 @@
             k_rows, qs[...], (((1,), (1,)), ((), ())), preferred_element_type=jnp.float32)
         shape = (nx, HALF, rows)
         raw = raw.reshape(shape) + bias[row]
-        key_at = (
-            (row * nx + lax.broadcasted_iota(jnp.int32, shape, 0)) * BLK
-            + core * HALF + lax.broadcasted_iota(jnp.int32, shape, 1))
-        query_at = s * BLK + lax.broadcasted_iota(jnp.int32, shape, 2) % BLK
-        raw = jnp.where(key_at <= query_at, raw, LOW).reshape(chunk, rows)
+        if diagonal:
+            key_at = (
+                (row * nx + lax.broadcasted_iota(jnp.int32, shape, 0)) * BLK
+                + core * HALF + lax.broadcasted_iota(jnp.int32, shape, 1))
+            query_at = s * BLK + lax.broadcasted_iota(jnp.int32, shape, 2) % BLK
+            raw = jnp.where(key_at <= query_at, raw, LOW)
+        raw = raw.reshape(chunk, rows)
         old = top[...]
         new = jnp.maximum(old, jnp.max(raw, axis=0, keepdims=True))
         w = jnp.exp2((raw - new) * SCALE2)
@@ -195,31 +197,38 @@
             lanes = slice(c * mine, (c + 1) * mine)
             part[c, :HD, :] = part[c, :HD, :] * keep[:, lanes] + more[:, lanes]
 
-    def one_row(row):
+    def one_row(row, diagonal=False):
         for u in sides:
             block_wait(row * nx + (x + u) % nx)
         if across:
             @pl.when((row < y) | (core == 1))
             def _():
                 block_wait(row * nx + (x + across) % nx)
-        attend(row)
-
-    below(one_row, 0)
+        attend(row, diagonal)
+
+    one_row(y, True)
+    below(one_row, 1)
 
     for c in range(2):
         lanes = slice(c * mine, (c + 1) * mine)
         part[c, HD : HD + 8, :] = jnp.broadcast_to(top[:, lanes], (8, mine))
         part[c, HD + 8 :, :] = jnp.broadcast_to(total[:, lanes], (8, mine))
-    part_copy = remote(part.at[1 - core], got, part_sem.at[0], part_sem.at[1], (s, sib))
-    part_copy.start()
-    part_copy.wait_recv()
-    top_a, top_b = part[core, HD : HD + 1, :], got[HD : HD + 1, :]
-    both = jnp.maximum(top_a, top_b)
-    scale_a = jnp.exp2((top_a - both) * SCALE2)
-    scale_b = jnp.exp2((top_b - both) * SCALE2)
-    under = part[core, HD + 8 : HD + 9, :] * scale_a + got[HD + 8 : HD + 9, :] * scale_b
-    mixed = (part[core, :HD, :] * scale_a + got[:HD, :] * scale_b) / under
-    gath[z] = mixed.T.astype(jnp.bfloat16).reshape(OWN, BLK, HD)
+    def part_copy(i):
+        lanes = pl.ds(i * (mine // 2), mine // 2)
+        return remote(part.at[1 - core, :, lanes], got.at[:, lanes], part_sem.at[0, i], part_sem.at[1, i], (s, sib))
+
+    for i in range(2):
+        part_copy(i).start()
+    for i in range(2):
+        lanes = slice(i * (mine // 2), (i + 1) * (mine // 2))
+        part_copy(i).wait_recv()
+        top_a, top_b = part[core, HD : HD + 1, lanes], got[HD : HD + 1, lanes]
+        both = jnp.maximum(top_a, top_b)
+        scale_a = jnp.exp2((top_a - both) * SCALE2)
+        scale_b = jnp.exp2((top_b - both) * SCALE2)
+        under = part[core, HD + 8 : HD + 9, lanes] * scale_a + got[HD + 8 : HD + 9, lanes] * scale_b
+        mixed = part[core, :HD, lanes] * (scale_a / under) + got[:HD, lanes] * (scale_b / under)
+        gath[z, i * 2 : i * 2 + 2] = mixed.T.astype(jnp.bfloat16).reshape(2, BLK, HD)
 
     top_edge, low_edge = nz - 1, ne
     edges = [sorted({0, ne - 1}), sorted({low_edge, top_edge})]
@@ -315,9 +324,7 @@
     collect(pick, sib)
     rest_copy = remote(pick, rest, rest_sem.at[0], rest_sem.at[1], (s, sib))
     rest_copy.start()
-    collect(own, h)
-    own_copy = pltpu.make_async_copy(own, out, in_sem.at[0])
-    own_copy.start()
+    collect(out, h)
 
     if across:
         across_copy.wait_send()
@@ -336,7 +343,8 @@
             x_copy(row, side).wait_send()
 
     below(left, 0)
-    part_copy.wait_send()
+    for i in range(2):
+        part_copy(i).wait_send()
 
     @pl.when(early)
     def _():
@@ -359,7 +367,6 @@
         def _():
             pass_copy(of, target, lane).wait_send()
     rest_copy.wait()
-    own_copy.wait()
 
 
 def per_device(nx, queries, keys, values, vertical, slash, plan):
@@ -374,9 +381,9 @@
     tables = (vertical.shape[1], vertical.shape[0])
     out, rest = pl.pallas_call(
         functools.partial(kernel, ny, nx, nz),
-        out_shape=[jax.ShapeDtypeStruct((BLK, OWN * HD), bf)] * 2,
+        out_shape=[pltpu.VMEM((BLK, OWN * HD), bf)] * 2,
         in_specs=[hbm] * 6,
-        out_specs=[hbm] * 2,
+        out_specs=[pl.BlockSpec(memory_space=pltpu.VMEM)] * 2,
         scratch_shapes=[
             pltpu.SMEM(plan.shape, jnp.int32),
             pltpu.VMEM(tables, jnp.int32),
@@ -391,7 +398,6 @@
             pltpu.VMEM((HD + 16, mine), f32),
             pltpu.VMEM((nz, OWN, BLK, HD), bf),
             pltpu.VMEM((BLK, OWN * HD), bf),
-            pltpu.VMEM((BLK, OWN * HD), bf),
             dma((6,)),
             dma((ny,)),
             dma((ny,)),
@@ -399,7 +405,7 @@
             dma((ny, 2)),
             dma((nb,)),
             dma((2,)),
-            dma((2,)),
+            dma((2, 2)),
             dma((nz,)),
             dma((2, nz)),
             dma((nz,)),

time: 39.4 us -> 38.5 us (0.977)
  other arithmetic: 1.52 us -> 0.65 us
    add x1, other arithmetic: 1.52 us -> 0.65 us  [per_device(): return out + rest]
where the time goes in v4:
time: 38.5 us; the launch traced here: 38.3 us
  Pallas kernels  37.6 us (98%)
  other arithmetic  0.65 us (2%)
    pallas_call x1, Pallas kernels, per_device(): pl.pallas_call(functools.partial(kernel, ny, nx, nz), out_shape=[pltpu.VM...  37.6 us

profile of v4, /device:TPU:57, one launch (start us, length us, event | category | flops | bytes accessed | tf_op | source)
XLA Modules:
  0.0 38.3 jit_solution(18126942854396914458)
XLA Ops:
  0.0 37.6 %shard_map.64 = (bf16[64,512]{1,0:T(8,128)(2,1)S(1)}, bf16[64,512]{1,0:T(8,128)(2,1)S(1)}) custom-call(s32[64]{0:T(128)} %plan_hbm.1, s32[8,64]{1,0:T(8,128)} %bitcast.2, s32[8,64]{1,0:T(8,128)} %bitcast.3, bf16[64,512]{1,0:T(8,128)(2,1)} %queries.1, bf16[64,1024]{1,0:T(8,128)(2,1)} %keys.1, bf16[64,1024]{1,0:T(8,128)(2,1)} %values.1), custom_call_target="tpu_custom_call" | custom-call | tf_op jit(solution)/shard_map/pallas_call | solution.py:382
  37.6 0.6 %add.3 = bf16[64,512]{1,0:T(8,128)(2,1)} add(bf16[64,512]{1,0:T(8,128)(2,1)S(1)} %get-tuple-element.7, bf16[64,512]{1,0:T(8,128)(2,1)S(1)} %get-tuple-element.8) | non-fusion elementwise | flops 32768 | bytes 196608 | tf_op jit(solution)/shard_map/add | solution.py:418

commit v5 on v4

--- a/solution.py
+++ b/solution.py
@@ -13,6 +13,7 @@
 NX = 4
 GROUP = 8
 OWN = 4
+PIECES = 2
 LOW = -1e30
 SCALE2 = (HD**-0.5) * 1.4426950408889634
 MESH = pl.DeviceIdType.MESH
@@ -53,24 +54,22 @@
     vert_load = pltpu.make_async_copy(vertical_hbm, vertical, in_sem.at[4])
     slash_load = pltpu.make_async_copy(slash_hbm, slash, in_sem.at[5])
     loads = [k_load, v_load, q_load, vert_load, slash_load, plan_load]
-    for load in loads:
-        load.start()
-
     barrier = pltpu.get_barrier_semaphore()
+    def greet(row, carry):
+        signal(barrier, (row * nx + x, h))
+        return carry
+
+    lax.fori_loop(0, y, greet, 0)
     partners = [(y * nx + (x + t) % nx, h) for t in range(1, nx)]
     partners += [(s, sib)]
     for partner in partners:
         signal(barrier, partner)
-
-    def greet(row, carry):
-        signal(barrier, (row * nx + x, h))
-        return carry
-
-    lax.fori_loop(0, y, greet, 0)
     for other in range(1, nz):
         @pl.when(other > z)
         def _():
             signal(barrier, (s, other * 2 + core))
+    for load in loads:
+        load.start()
     pl.semaphore_wait(barrier, len(partners) + ny - 1 - y + z)
 
     def y_copy(t):
@@ -217,6 +216,15 @@
         lanes = pl.ds(i * (mine // 2), mine // 2)
         return remote(part.at[1 - core, :, lanes], got.at[:, lanes], part_sem.at[0, i], part_sem.at[1, i], (s, sib))
 
+    width = OWN // PIECES
+
+    def send(source, target, sem, piece):
+        block = gath.at[source, pl.ds(piece * width, width)]
+        return remote(block, block, sem, z_recv.at[source, piece], (s, target * 2 + core))
+
+    high = z >= nz - ne // 2
+    nearer = jnp.where(high, 0, ne - 1)
+
     for i in range(2):
         part_copy(i).start()
     for i in range(2):
@@ -230,30 +238,36 @@
         mixed = part[core, :HD, lanes] * (scale_a / under) + got[:HD, lanes] * (scale_b / under)
         gath[z, i * 2 : i * 2 + 2] = mixed.T.astype(jnp.bfloat16).reshape(2, BLK, HD)
 
+        @pl.when(jnp.logical_not(early))
+        def _():
+            send(z, nearer, z_send.at[0, i], i).start()
+
     top_edge, low_edge = nz - 1, ne
     edges = [sorted({0, ne - 1}), sorted({low_edge, top_edge})]
     passes = ne >= 4
     upper = range(nz - ne // 2, nz) if passes else []
     lower = [source for source in range(ne, nz) if source not in upper]
 
-    def send(source, target, sem):
-        return remote(gath.at[source], gath.at[source], sem, z_recv.at[source], (s, target * 2 + core))
-
-    def z_copy(target):
-        return send(z, target, z_send.at[target])
-
-    def pass_copy(source, target, lane=0):
-        return send(source, target, pass_send.at[lane, source])
+    def z_start(target, slot):
+        for piece in range(PIECES):
+            send(z, target, z_send.at[slot, piece], piece).start()
+
+    def z_left(slot):
+        for piece in range(PIECES):
+            send(z, 0, z_send.at[slot, piece], piece).wait_send()
+
+    def pass_copy(source, target, lane, piece):
+        return send(source, target, pass_send.at[lane, source, piece], piece)
 
     def late_wait(target):
         @pl.when(target > z)
         def _():
             pl.semaphore_wait(late.at[target], 1)
 
-    def arrive(source):
+    def arrive(source, piece):
         @pl.when(source != z)
         def _():
-            pass_copy(source, 0).wait_recv()
+            pass_copy(source, 0, 0, piece).wait_recv()
 
     routes = []
     if passes:
@@ -265,13 +279,17 @@
         routes += [(low_edge, source, low_edge + 1, 0) for source in range(ne)]
 
     def relay(plane, order):
+        pairs = [order[i : i + 2] for i in range(0, len(order), 2)]
+
         @pl.when(z == plane)
         def _():
-            for source in order:
-                arrive(source)
-                for by, of, target, lane in routes:
-                    if by == plane and of == source:
-                        pass_copy(source, target, lane).start()
+            for pair in pairs:
+                for piece in range(PIECES):
+                    for source in pair:
+                        arrive(source, piece)
+                        for by, of, target, lane in routes:
+                            if by == plane and of == source:
+                                pass_copy(source, target, lane, piece).start()
 
     @pl.when(early)
     def _():
@@ -280,38 +298,35 @@
 
             @pl.when(target != z)
             def _():
-                z_copy(target).start()
+                z_start(target, target)
         for target in reversed(range(ne, nz)):
             late_wait(target)
             if target in edges[1]:
-                z_copy(target).start()
+                z_start(target, target)
         for source in range(ne):
-            arrive(source)
+            for piece in range(PIECES):
+                arrive(source, piece)
         relay(0, list(reversed(range(ne, nz))))
         for plane in range(1, ne):
             relay(plane, list(range(ne, nz)))
 
     @pl.when(jnp.logical_not(early))
     def _():
-        high = z >= nz - ne // 2
         if len(edges[0]) == 2:
-            first = jnp.where(high, 0, ne - 1)
-            second = ne - 1 - first
-            send(z, first, z_send.at[0]).start()
+            second = ne - 1 - nearer
             for target in range(ne, nz):
                 late_wait(target)
 
                 @pl.when(target != z)
                 def _():
-                    z_copy(target).start()
-            z_copy(0).wait_send()
-            send(z, second, z_send.at[1]).start()
-        else:
-            send(z, 0, z_send.at[0]).start()
+                    z_start(target, target)
+            z_left(0)
+            z_start(second, 1)
         for plane in range(ne, nz):
             relay(plane, list(range(ne)))
         for source in range(ne, nz):
-            arrive(source)
+            for piece in range(PIECES):
+                arrive(source, piece)
 
     plan_load.wait()
 
@@ -351,21 +366,22 @@
         for target in range(ne):
             @pl.when(target != z)
             def _():
-                z_copy(target).wait_send()
+                z_left(target)
         for target in edges[1]:
-            z_copy(target).wait_send()
+            z_left(target)
 
     @pl.when(jnp.logical_not(early))
     def _():
-        z_copy(len(edges[0]) - 1).wait_send()
+        z_left(len(edges[0]) - 1)
         for target in range(ne, nz):
             @pl.when(target != z)
             def _():
-                z_copy(target).wait_send()
+                z_left(target)
     for by, of, target, lane in routes:
         @pl.when(z == by)
         def _():
-            pass_copy(of, target, lane).wait_send()
+            for piece in range(PIECES):
+                pass_copy(of, target, lane, piece).wait_send()
     rest_copy.wait()
 
 
@@ -406,9 +422,9 @@
             dma((nb,)),
             dma((2,)),
             dma((2, 2)),
-            dma((nz,)),
-            dma((2, nz)),
-            dma((nz,)),
+            dma((nz, PIECES)),
+            dma((2, nz, PIECES)),
+            dma((nz, PIECES)),
             dma((2,)),
             pltpu.SemaphoreType.REGULAR((nz,)),
         ],

time: 38.5 us -> 38.6 us (level)
  no operation moved by 1% of the time
where the time goes in v5:
time: 38.6 us; the launch traced here: 38.5 us
  Pallas kernels  37.8 us (98%)
  other arithmetic  0.65 us (2%)
    pallas_call x1, Pallas kernels, per_device(): pl.pallas_call(functools.partial(kernel, ny, nx, nz), out_shape=[pltpu.VM...  37.8 us

profile of v5, /device:TPU:57, one launch (start us, length us, event | category | flops | bytes accessed | tf_op | source)
XLA Modules:
  0.0 38.5 jit_solution(1081286056890091456)
XLA Ops:
  0.0 37.8 %shard_map.64 = (bf16[64,512]{1,0:T(8,128)(2,1)S(1)}, bf16[64,512]{1,0:T(8,128)(2,1)S(1)}) custom-call(s32[64]{0:T(128)} %plan_hbm.1, s32[8,64]{1,0:T(8,128)} %bitcast.2, s32[8,64]{1,0:T(8,128)} %bitcast.3, bf16[64,512]{1,0:T(8,128)(2,1)} %queries.1, bf16[64,1024]{1,0:T(8,128)(2,1)} %keys.1, bf16[64,1024]{1,0:T(8,128)(2,1)} %values.1), custom_call_target="tpu_custom_call" | custom-call | tf_op jit(solution)/shard_map/pallas_call | solution.py:398
  37.8 0.6 %add.3 = bf16[64,512]{1,0:T(8,128)(2,1)} add(bf16[64,512]{1,0:T(8,128)(2,1)S(1)} %get-tuple-element.7, bf16[64,512]{1,0:T(8,128)(2,1)S(1)} %get-tuple-element.8) | non-fusion elementwise | flops 32768 | bytes 196608 | tf_op jit(solution)/shard_map/add | solution.py:434

commit v6 on v4

--- a/solution.py
+++ b/solution.py
@@ -53,24 +53,22 @@
     vert_load = pltpu.make_async_copy(vertical_hbm, vertical, in_sem.at[4])
     slash_load = pltpu.make_async_copy(slash_hbm, slash, in_sem.at[5])
     loads = [k_load, v_load, q_load, vert_load, slash_load, plan_load]
-    for load in loads:
-        load.start()
-
     barrier = pltpu.get_barrier_semaphore()
+    def greet(row, carry):
+        signal(barrier, (row * nx + x, h))
+        return carry
+
+    lax.fori_loop(0, y, greet, 0)
     partners = [(y * nx + (x + t) % nx, h) for t in range(1, nx)]
     partners += [(s, sib)]
     for partner in partners:
         signal(barrier, partner)
-
-    def greet(row, carry):
-        signal(barrier, (row * nx + x, h))
-        return carry
-
-    lax.fori_loop(0, y, greet, 0)
     for other in range(1, nz):
         @pl.when(other > z)
         def _():
             signal(barrier, (s, other * 2 + core))
+    for load in loads:
+        load.start()
     pl.semaphore_wait(barrier, len(partners) + ny - 1 - y + z)
 
     def y_copy(t):
@@ -260,7 +258,7 @@
         for source in upper:
             routes += [(0, source, 1, 0), (0, source, ne - 2, 1)]
         for source in lower:
-            routes += [(ne - 1, source, ne - 2, 0), (ne - 1, source, 1, 1)]
+            routes += [(ne - 1, source, 1, 1), (ne - 1, source, ne - 2, 0)]
         routes += [(top_edge, source, top_edge - 1, 0) for source in range(ne)]
         routes += [(low_edge, source, low_edge + 1, 0) for source in range(ne)]
 

time: 38.5 us -> 38.5 us (level)
  no operation moved by 1% of the time
where the time goes in v6:
time: 38.5 us; the launch traced here: 38.2 us
  Pallas kernels  37.6 us (98%)
  other arithmetic  0.65 us (2%)
    pallas_call x1, Pallas kernels, per_device(): pl.pallas_call(functools.partial(kernel, ny, nx, nz), out_shape=[pltpu.VM...  37.6 us

profile of v6, /device:TPU:57, one launch (start us, length us, event | category | flops | bytes accessed | tf_op | source)
XLA Modules:
  0.0 38.2 jit_solution(13091342822541579630)
XLA Ops:
  0.0 37.6 %shard_map.64 = (bf16[64,512]{1,0:T(8,128)(2,1)S(1)}, bf16[64,512]{1,0:T(8,128)(2,1)S(1)}) custom-call(s32[64]{0:T(128)} %plan_hbm.1, s32[8,64]{1,0:T(8,128)} %bitcast.2, s32[8,64]{1,0:T(8,128)} %bitcast.3, bf16[64,512]{1,0:T(8,128)(2,1)} %queries.1, bf16[64,1024]{1,0:T(8,128)(2,1)} %keys.1, bf16[64,1024]{1,0:T(8,128)(2,1)} %values.1), custom_call_target="tpu_custom_call" | custom-call | tf_op jit(solution)/shard_map/pallas_call | solution.py:380
  37.6 0.6 %add.3 = bf16[64,512]{1,0:T(8,128)(2,1)} add(bf16[64,512]{1,0:T(8,128)(2,1)S(1)} %get-tuple-element.7, bf16[64,512]{1,0:T(8,128)(2,1)S(1)} %get-tuple-element.8) | non-fusion elementwise | flops 32768 | bytes 196608 | tf_op jit(solution)/shard_map/add | solution.py:416
